TPU v7x, 32 devices: a whole 2x2x4 slice. The times are simulated.
32 devices in a mesh: group: 2 (over y), dec: 16 (over z, x, core).
Axes of the slice: x: 2, y: 2, z: 4, core: 2. Of those that a mesh axis runs over, the one named last changes fastest.
Arguments:
- image_states: bfloat16 [56, 256, 8192], P('group', 'dec'), parts along dimension 0, may hold values from -6 to 6
- w_key: bfloat16 [8192, 512], P('dec'), may hold values from -0.0625 to 0.0625
- w_value: bfloat16 [8192, 512], P('dec'), may hold values from -0.25 to 0.25
- key_gain: float32 [128], replicated, may hold values from 0.5 to 2
- query_gain: float32 [128], replicated, may hold values from 0.5 to 2
- head_gate: float32 [32], replicated, may hold values from 0.3 to 2
- queries: bfloat16 [32, 256, 4096], P(('group', 'dec')), parts along dimension 0, may hold values from -6 to 6
- tile_counts: int32 [32], P('group'), parts along dimension 0, may hold values from 1 to 4, 28 in all
- owner_of: int32 [32], P('group'), parts along dimension 0, may hold values from 0 to 15, each once
Outputs:
- attended: bfloat16 [32, 256, 4096], P(('group', 'dec')), parts along dimension 0
There are 2 independent parts, one for each index of `group`. A program takes and returns all parts, laid end to end along the dimension named above; an argument that names none is the same for every part. Nothing has to cross between parts.
Inputs may be any that keep to these rules, and one draw needn't show every extreme that they name: `tile_counts`: the counts sum to 28; some request has exactly 4 tiles. `owner_of`: every device index appears exactly once.
All inputs are finite; a program needn't handle non-finite values.
Results may differ from a plain program's by a relative error of at most 0.0087.
Values may be sent and summed in bfloat16 or wider, within the bound.
A program may use at most 128 MiB of HBM per device.

v0:
```python
import math

import jax
import jax.numpy as jnp
from jax import lax
from jax.sharding import PartitionSpec as P

MAX_TILES = 4


EPS = 1e-05


def rms_scale(values, gain):
    mean_square = jnp.mean(values * values, axis=-1, keepdims=True)
    return values * lax.rsqrt(mean_square + EPS) * gain


def project_rows(states, w_key, w_value, key_gain, kv_heads):
    leading = states.shape[:-1]
    width = w_key.shape[1]
    head_size = width // kv_heads
    flat_rows = states.reshape(-1, states.shape[-1])
    key_sum = jnp.dot(
        flat_rows,
        lax.all_gather(w_key, "dec", axis=0, tiled=True),
        preferred_element_type=jnp.float32,
    )
    value_sum = jnp.dot(
        flat_rows,
        lax.all_gather(w_value, "dec", axis=0, tiled=True),
        preferred_element_type=jnp.float32,
    )
    key_heads = key_sum.reshape(-1, kv_heads, head_size)
    key_rows = rms_scale(key_heads, key_gain).astype(jnp.bfloat16).reshape(leading + (width,))
    value_rows = value_sum.astype(jnp.bfloat16).reshape(leading + (width,))
    return (key_rows, value_rows)


def attend_slots(query_norm, key_blocks, value_blocks):
    kv_heads = query_norm.shape[1]
    head_size = query_norm.shape[-1]
    slot_total = key_blocks.shape[0]
    key_heads = jnp.moveaxis(key_blocks.reshape(slot_total, -1, kv_heads, head_size), 2, 0)
    value_heads = jnp.moveaxis(value_blocks.reshape(slot_total, -1, kv_heads, head_size), 2, 0)
    query_heads = jnp.moveaxis(query_norm, 1, 0)

    def one_head(item):
        query_part, key_part, value_part = item
        scores = jnp.einsum(
            "tgh,mkh->mgtk", query_part, key_part, preferred_element_type=jnp.float32
        ) / math.sqrt(head_size)
        weights = jnp.exp(scores)
        totals = jnp.sum(weights, axis=-1)
        accum = jnp.einsum(
            "mgtk,mkh->mtgh",
            weights.astype(jnp.bfloat16),
            value_part,
            preferred_element_type=jnp.float32,
        )
        return (totals, accum)

    totals, accum = lax.map(one_head, (query_heads, key_heads, value_heads))
    return (jnp.moveaxis(totals, 0, 1), jnp.moveaxis(accum, 0, 2))


def body(
    image_states, w_key, w_value, key_gain, query_gain, head_gate, queries, tile_counts, owner_of
):
    own_index = lax.axis_index("dec")
    tiles_total = image_states.shape[0]
    head_size = key_gain.shape[0]
    kv_heads = w_key.shape[1] // head_size
    text_len = queries.shape[1]
    group_size = queries.shape[2] // (kv_heads * head_size)
    request_ids = jnp.arange(owner_of.shape[0], dtype=jnp.int32)
    owned = owner_of[None, :] == request_ids[:, None]
    tile_starts = jnp.cumsum(tile_counts) - tile_counts
    peer_counts = jnp.sum(jnp.where(owned, tile_counts[None, :], 0), axis=1)
    peer_starts = jnp.sum(jnp.where(owned, tile_starts[None, :], 0), axis=1)
    slot_ids = jnp.arange(MAX_TILES, dtype=jnp.int32)
    wanted = jnp.minimum(peer_starts[None, :] + slot_ids[:, None], tiles_total - 1)
    in_use = slot_ids[:, None] < peer_counts[None, :]

    def pack(source):
        picked = jnp.take(source, wanted, axis=0)
        return jnp.where(in_use[:, :, None, None], picked, jnp.zeros((), source.dtype))

    own_count = jnp.sum(jnp.where(request_ids == own_index, peer_counts, 0))
    query_rows = queries[0].astype(jnp.float32).reshape(text_len, kv_heads, group_size, head_size)
    query_norm = rms_scale(query_rows, query_gain).astype(jnp.bfloat16)
    key_rows, value_rows = project_rows(image_states, w_key, w_value, key_gain, kv_heads)
    outgoing = (pack(key_rows), pack(value_rows))
    received = (
        lax.all_to_all(outgoing[0], "dec", split_axis=1, concat_axis=1, tiled=True),
        lax.all_to_all(outgoing[1], "dec", split_axis=1, concat_axis=1, tiled=True),
    )
    totals, accum = attend_slots(query_norm, received[0], received[1])
    slot_live = (slot_ids < own_count).astype(jnp.float32)
    total_sum = jnp.sum(totals * slot_live[:, None, None, None], axis=0)
    accum_sum = jnp.sum(accum * slot_live[:, None, None, None, None], axis=0)
    gate_value = jnp.tanh(head_gate).reshape(kv_heads, group_size)
    mixed = (
        accum_sum
        / jnp.transpose(total_sum, (2, 0, 1))[:, :, :, None]
        * gate_value[None, :, :, None]
    )
    return mixed.reshape(text_len, kv_heads * group_size * head_size).astype(jnp.bfloat16)[None]


def solution(mesh):
    placed = (
        P("group", "dec", None),
        P("dec", None),
        P("dec", None),
        P(),
        P(),
        P(),
        P(("group", "dec"), None, None),
        P("group"),
        P("group"),
    )
    return jax.shard_map(
        body, mesh=mesh, in_specs=placed, out_specs=P(("group", "dec"), None, None), check_vma=False
    )
```

profile of v0, /device:TPU:11, one launch (start us, length us, event | category | flops | bytes accessed | tf_op | source)
XLA Modules:
  0.0 290.8 jit_solution(16296759221397065158)
XLA Ops:
  6.5 0.7 all-gather.3.cloned.1.call-update
  7.3 0.7 all-gather.5.cloned.1.call-update
  8.0 0.7 copy.49
  9.6 0.8 select_reduce_fusion.1
  10.5 74.0 %all-gather.3.cloned.1.call-done = bf16[8192,512]{1,0:T(8,128)(2,1)} async-done(((bf16[512,512]{1,0:T(8,128)(2,1)}), bf16[8192,512]{1,0:T(8,128)(2,1)}) %all-gather.3.cloned.1.call-update) | async-done | bytes 8388624 | tf_op jit(solution)/shard_map/all_gather | solution.py:26
  84.5 11.3 %copy.50 = bf16[512,8192]{1,0:T(8,128)(2,1)} copy(bf16[512,8192]{0,1:T(8,128)(2,1)} %bitcast.79) | data formatting | bytes 16777216 | tf_op jit(solution)/shard_map/dot_general | solution.py:24
  95.8 8.0 %multiply_reduce_fusion.1 = (f32[448,4]{0,1:T(4,128)S(1)}, f32[448,4,128]{2,0,1:T(8,128)S(1)}) fusion(bf16[448,8192,1]{1,0,2:T(8,128)(2,1)} %bitcast.88, bf16[4,128,8192]{2,1,0:T(8,128)(2,1)} %bitcast.80), kind=kOutput, calls=%fused_computation.32 | convolution fusion | flops 3758553344 | bytes 16653312 | tf_op jit(solution)/shard_map/dot_general | solution.py:24
  104.7 55.1 %all-gather.5.cloned.1.call-done = bf16[8192,512]{1,0:T(8,128)(2,1)} async-done(((bf16[512,512]{1,0:T(8,128)(2,1)}), bf16[8192,512]{1,0:T(8,128)(2,1)}) %all-gather.5.cloned.1.call-update) | async-done | bytes 8388624 | tf_op jit(solution)/shard_map/all_gather | solution.py:31
  159.8 9.4 %convolution_convert_fusion = bf16[448,512]{1,0:T(8,128)(2,1)S(1)} fusion(bf16[448,8192]{1,0:T(8,128)(2,1)} %bitcast.89, bf16[8192,512]{1,0:T(8,128)(2,1)} %all-gather.5.cloned.1.call-done), kind=kOutput, calls=%fused_computation.28 | convolution fusion | flops 3758325760 | bytes 16187392 | tf_op jit(solution)/shard_map/dot_general | solution.py:29
  170.5 1.3 select_select_fusion
  171.8 1.1 copy.52
  172.9 5.4 %all-to-all-start = ((bf16[4,16,16,512]{3,2,0,1:T(8,128)(2,1)}), bf16[4,16,16,512]{3,2,0,1:T(8,128)(2,1)S(1)}, u32[]{:S(2)}, u32[]{:S(2)}) async-start(bf16[4,16,16,512]{3,2,0,1:T(8,128)(2,1)} %copy.52), calls=%async_computation | async-start | bytes 2097152 | tf_op jit(solution)/shard_map/all_to_all | solution.py:95
  178.3 2.3 copy.55
  180.6 22.6 %all-to-all-done = bf16[4,16,16,512]{3,2,0,1:T(8,128)(2,1)S(1)} async-done(((bf16[4,16,16,512]{3,2,0,1:T(8,128)(2,1)}), bf16[4,16,16,512]{3,2,0,1:T(8,128)(2,1)S(1)}, u32[]{:S(2)}, u32[]{:S(2)}) %all-to-all-start) | async-done | bytes 1048608 | tf_op jit(solution)/shard_map/all_to_all | solution.py:95
  203.2 4.9 %all-to-all-start.1 = ((bf16[4,16,16,512]{3,2,0,1:T(8,128)(2,1)}), bf16[4,16,16,512]{3,2,0,1:T(8,128)(2,1)}, u32[]{:S(2)}, u32[]{:S(2)}) async-start(bf16[4,16,16,512]{3,2,0,1:T(8,128)(2,1)} %copy.55), calls=%async_computation.1 | async-start | bytes 2097152 | tf_op jit(solution)/shard_map/all_to_all | solution.py:96
  208.1 3.3 %copy.54 = bf16[1,256,4096]{1,2,0:T(8,128)(2,1)S(1)} copy(bf16[1,256,4096]{2,1,0:T(8,128)(2,1)} %param.19) | data formatting | bytes 4194304 | tf_op args[6]
  213.4 2.1 fusion.15
  216.0 17.0 %all-to-all-done.1 = bf16[4,16,16,512]{3,2,0,1:T(8,128)(2,1)} async-done(((bf16[4,16,16,512]{3,2,0,1:T(8,128)(2,1)}), bf16[4,16,16,512]{3,2,0,1:T(8,128)(2,1)}, u32[]{:S(2)}, u32[]{:S(2)}) %all-to-all-start.1) | async-done | bytes 1048608 | tf_op jit(solution)/shard_map/all_to_all | solution.py:96
  233.1 1.3 copy.56
  235.4 24.0 %while.12 = (s32[]{:T(128)}, f32[4,4,8,256]{3,2,1,0:T(8,128)S(1)}, f32[4,4,256,8,128]{2,4,3,1,0:T(8,128)}, bf16[4,4,256,128]{3,2,1,0:T(8,128)(2,1)S(1)}, bf16[4,...) while((s32[]{:T(128)}, f32[4,4,8,256]{3,2,1,0:T(8,128)S(1)}, ...), condition=%wide.region_7.9_spmd, body=%wide.region_5.8_spmd.sunk | while | flops 1082122240 | bytes 22120536 | solution.py:63
  235.4 2.5 bitcast_reduce_fusion.2
  237.9 3.5 %bitcast_dynamic-update-slice_fusion.5 = f32[4,4,256,8,128]{2,4,3,1,0:T(8,128)} fusion(f32[4,4,256,8,128]{2,4,3,1,0:T(8,128)} %get-tuple-element.137, s32[]{:T(128)S(6)} %copy.70, f32[4,256,256,8]{2,1,3,0:T(8,128)S(1)} %get-tuple-element.127, bf16[4,4,256,128]{2,3,1,0:T(8,128)(2,1)S(1)} %get-tuple-element.147), kind=kOutput, calls=%fused_computation.6.clone.1 | convolution fusion | flops 541065216 | bytes 12846080 | tf_op jit(solution)/shard_map/while/body/eval_jaxpr/mgtk,mkh->mtgh/dot_general | solution.py:55
  241.4 2.4 bitcast_reduce_fusion.2
  243.8 3.5 %bitcast_dynamic-update-slice_fusion.5 = f32[4,4,256,8,128]{2,4,3,1,0:T(8,128)} fusion(f32[4,4,256,8,128]{2,4,3,1,0:T(8,128)} %get-tuple-element.137, s32[]{:T(128)S(6)} %copy.70, f32[4,256,256,8]{2,1,3,0:T(8,128)S(1)} %get-tuple-element.127, bf16[4,4,256,128]{2,3,1,0:T(8,128)(2,1)S(1)} %get-tuple-element.147), kind=kOutput, calls=%fused_computation.6.clone.1 | convolution fusion | flops 541065216 | bytes 12846080 | tf_op jit(solution)/shard_map/while/body/eval_jaxpr/mgtk,mkh->mtgh/dot_general | solution.py:55
  247.4 2.4 bitcast_reduce_fusion.2
  249.8 3.5 %bitcast_dynamic-update-slice_fusion.5 = f32[4,4,256,8,128]{2,4,3,1,0:T(8,128)} fusion(f32[4,4,256,8,128]{2,4,3,1,0:T(8,128)} %get-tuple-element.137, s32[]{:T(128)S(6)} %copy.70, f32[4,256,256,8]{2,1,3,0:T(8,128)S(1)} %get-tuple-element.127, bf16[4,4,256,128]{2,3,1,0:T(8,128)(2,1)S(1)} %get-tuple-element.147), kind=kOutput, calls=%fused_computation.6.clone.1 | convolution fusion | flops 541065216 | bytes 12846080 | tf_op jit(solution)/shard_map/while/body/eval_jaxpr/mgtk,mkh->mtgh/dot_general | solution.py:55
  253.4 2.4 bitcast_reduce_fusion.2
  255.9 3.5 %bitcast_dynamic-update-slice_fusion.5 = f32[4,4,256,8,128]{2,4,3,1,0:T(8,128)} fusion(f32[4,4,256,8,128]{2,4,3,1,0:T(8,128)} %get-tuple-element.137, s32[]{:T(128)S(6)} %copy.70, f32[4,256,256,8]{2,1,3,0:T(8,128)S(1)} %get-tuple-element.127, bf16[4,4,256,128]{2,3,1,0:T(8,128)(2,1)S(1)} %get-tuple-element.147), kind=kOutput, calls=%fused_computation.6.clone.1 | convolution fusion | flops 541065216 | bytes 12846080 | tf_op jit(solution)/shard_map/while/body/eval_jaxpr/mgtk,mkh->mtgh/dot_general | solution.py:55
  259.4 10.3 %multiply_reduce_fusion = f32[4,256,8,128]{1,3,2,0:T(8,128)} fusion(f32[4,4,256,8,128]{2,4,3,1,0:T(8,128)} %get-tuple-element.39, f32[4]{0:T(128)S(1)} %compare_convert_fusion), kind=kLoop, calls=%fused_computation.19 | loop fusion | flops 7340032 | bytes 20971536 | tf_op jit(solution)/shard_map/reduce_sum | solution.py:101
  269.8 4.6 %bitcast_divide_fusion = f32[256,4,8,128]{0,3,2,1:T(8,128)} fusion(f32[4,256,8,128]{1,3,2,0:T(8,128)} %multiply_reduce_fusion, f32[256,4,8]{0,2,1:T(8,128)S(1)} %bitcast.86), kind=kLoop, calls=%fused_computation.25 | loop fusion | flops 1048576 | bytes 8421376 | tf_op jit(solution)/shard_map/div | solution.py:104
  274.5 5.6 %copy.60 = f32[1,256,4096]{2,1,0:T(8,128)} copy(f32[1,256,4096]{1,2,0:T(8,128)} %bitcast.78) | data formatting | bytes 8388608 | tf_op jit(solution)/shard_map/div | solution.py:104
  280.1 3.9 %multiply_convert_fusion = bf16[1,256,4096]{2,1,0:T(8,128)(2,1)} fusion(f32[1,256,4096]{2,1,0:T(8,128)} %copy.60, f32[4096]{0:T(1024)S(1)} %broadcast_bitcast_fusion), kind=kLoop, calls=%fused_computation.26 | loop fusion | flops 2097152 | bytes 6307840 | tf_op jit(solution)/shard_map/convert_element_type | solution.py:108
  (40 shorter events, 6.6 us)
Async XLA Ops:
  6.5 78.0 %all-gather.3.cloned.1.call-start = ((), (), s32[]{:S(2)}) async-start(), calls=%async_computation.2 | async-start | bytes 8912896 | tf_op jit(solution)/shard_map/all_gather | solution.py:26
  7.3 152.6 %all-gather.5.cloned.1.call-start = ((), (), s32[]{:S(2)}) async-start(), calls=%async_computation.3 | async-start | bytes 8912896 | tf_op jit(solution)/shard_map/all_gather | solution.py:31
  95.8 8.1 %copy-start = (f32[128]{0:T(128)S(1)}, f32[128]{0:T(128)}, u32[]{:S(2)}) copy-start(f32[128]{0:T(128)} %param.16) | copy-start | bytes 1540
  171.8 39.6 %copy-start.2 = (f32[32]{0:T(128)S(1)}, f32[32]{0:T(128)}, u32[]{:S(2)}) copy-start(f32[32]{0:T(128)} %param.18) | copy-start | bytes 388
  171.8 41.6 %copy-start.1 = (f32[128]{0:T(128)S(1)}, f32[128]{0:T(128)}, u32[]{:S(2)}) copy-start(f32[128]{0:T(128)} %param.17) | copy-start | bytes 1540
  172.9 30.3 %all-to-all-start = ((bf16[4,16,16,512]{3,2,0,1:T(8,128)(2,1)}), bf16[4,16,16,512]{3,2,0,1:T(8,128)(2,1)S(1)}, u32[]{:S(2)}, u32[]{:S(2)}) async-start(bf16[4,16,16,512]{3,2,0,1:T(8,128)(2,1)} %copy.52), calls=%async_computation | async-start | bytes 2097152 | tf_op jit(solution)/shard_map/all_to_all | solution.py:95
  203.2 29.9 %all-to-all-start.1 = ((bf16[4,16,16,512]{3,2,0,1:T(8,128)(2,1)}), bf16[4,16,16,512]{3,2,0,1:T(8,128)(2,1)}, u32[]{:S(2)}, u32[]{:S(2)}) async-start(bf16[4,16,16,512]{3,2,0,1:T(8,128)(2,1)} %copy.55), calls=%async_computation.1 | async-start | bytes 2097152 | tf_op jit(solution)/shard_map/all_to_all | solution.py:96
Sparse Core Ops, SparseCore 0:
  9.5 74.9 all-gather.2
  86.7 73.1 all-gather.4
where the time goes:
time: 292 us; the launch traced here: 291 us
  waiting for transfers between devices  170 us (58%)
  matrix products  41.3 us (14%)
  local copies, waits for them, and re-layouts  29.2 us (10%)
  other arithmetic  26 us (9%)
  between operations  13.6 us (5%)
  starting transfers between devices  10.4 us (4%)
    all_gather x1, waiting for transfers between devices, project_rows(): lax.all_gather(w_key, 'dec', axis=0, tiled=True)  74 us
    all_gather x1, waiting for transfers between devices, project_rows(): lax.all_gather(w_value, 'dec', axis=0, tiled=True)  55.1 us
    all_to_all x1, waiting for transfers between devices, body(): lax.all_to_all(outgoing[0], 'dec', split_axis=1, concat_axis=1, tiled=True)  22.6 us
    all_to_all x1, waiting for transfers between devices, body(): lax.all_to_all(outgoing[1], 'dec', split_axis=1, concat_axis=1, tiled=True)  17 us
    dot_general x4, matrix products, one_head(): jnp.einsum('mgtk,mkh->mtgh', weights.astype(jnp.bfloat16), value_part, pr...  14.1 us
    dot_general x1, local copies, waits for them, and re-layouts, project_rows(): jnp.dot(flat_rows, lax.all_gather(w_key, 'dec', axis=0, tiled=True), pref...  11.3 us
    reduce_sum x1, other arithmetic, body(): accum_sum = jnp.sum(accum * slot_live[:, None, None, None, None], axis=0)  10.3 us
    dot_general x4, matrix products, one_head(): jnp.einsum('tgh,mkh->mgtk', query_part, key_part, preferred_element_type=...  9.79 us
  transfers between devices with their start and end apart: 4, of which 4 were waited for; matrix products, arithmetic and copies ran while one was open for 11% of the time, Pallas kernels for 0%

commit v1 on v0

v1 whole, which is shorter than its diff:
```python
import functools
import math

import jax
import jax.numpy as jnp
from jax import lax
from jax.experimental import pallas as pl
from jax.experimental.pallas import tpu as pltpu
from jax.sharding import PartitionSpec as P

MAX_TILES = 4


EPS = 1e-05


def rms_scale(values, gain):
    mean_square = jnp.mean(values * values, axis=-1, keepdims=True)
    return values * lax.rsqrt(mean_square + EPS) * gain


def project_rows(states, w_key, w_value, key_gain, kv_heads):
    leading = states.shape[:-1]
    width = w_key.shape[1]
    head_size = width // kv_heads
    flat_rows = states.reshape(-1, states.shape[-1])
    key_sum = jnp.dot(
        flat_rows,
        lax.all_gather(w_key, "dec", axis=0, tiled=True),
        preferred_element_type=jnp.float32,
    )
    value_sum = jnp.dot(
        flat_rows,
        lax.all_gather(w_value, "dec", axis=0, tiled=True),
        preferred_element_type=jnp.float32,
    )
    key_heads = key_sum.reshape(-1, kv_heads, head_size)
    key_rows = rms_scale(key_heads, key_gain).astype(jnp.bfloat16).reshape(leading + (width,))
    value_rows = value_sum.astype(jnp.bfloat16).reshape(leading + (width,))
    return (key_rows, value_rows)


def attend_kernel(scale, head_size, q_ref, k_ref, v_ref, qgain_ref, gate_ref, live_ref, o_ref):
    slots = live_ref.shape[0]
    keys = k_ref.shape[0] // slots
    group_size = q_ref.shape[1] // head_size
    ones = jnp.ones((keys, head_size), jnp.bfloat16)
    gain = qgain_ref[...]
    blocks = []
    for j in range(slots):
        rows = pl.ds(j * keys, keys)
        blocks.append((k_ref[rows, :], jnp.concatenate([v_ref[rows, :], ones], axis=1)))
    for g in range(group_size):
        cols = pl.ds(g * head_size, head_size)
        q = q_ref[:, cols].astype(jnp.float32)
        q = rms_scale(q, gain).astype(jnp.bfloat16)
        acc = None
        for j in range(slots):
            key_block, value_block = blocks[j]
            scores = lax.dot_general(
                q, key_block, (((1,), (1,)), ((), ())), preferred_element_type=jnp.float32
            )
            weights = jnp.exp2(scores * scale).astype(jnp.bfloat16)
            part = jnp.dot(weights, value_block, preferred_element_type=jnp.float32)
            part = part * live_ref[j]
            acc = part if acc is None else acc + part
        gate = gate_ref[:, cols]
        o_ref[:, cols] = (acc[:, :head_size] / acc[:, head_size:] * gate).astype(o_ref.dtype)


def attend(queries, keys, values, query_gain, gates, live, head_size):
    text_len, width = queries.shape
    total = keys.shape[0]
    kv_heads = keys.shape[1] // head_size
    part = width // kv_heads
    scale = math.log2(math.e) / math.sqrt(head_size)
    return pl.pallas_call(
        functools.partial(attend_kernel, scale, head_size),
        grid=(kv_heads,),
        out_shape=jax.ShapeDtypeStruct((text_len, width), jnp.bfloat16),
        in_specs=[
            pl.BlockSpec((text_len, part), lambda h: (0, h)),
            pl.BlockSpec((total, head_size), lambda h: (0, h)),
            pl.BlockSpec((total, head_size), lambda h: (0, h)),
            pl.BlockSpec((1, head_size), lambda h: (0, 0)),
            pl.BlockSpec((1, part), lambda h: (0, h)),
            pl.BlockSpec(memory_space=pltpu.SMEM),
        ],
        out_specs=pl.BlockSpec((text_len, part), lambda h: (0, h)),
        compiler_params=pltpu.CompilerParams(vmem_limit_bytes=32 << 20),
    )(queries, keys, values, query_gain, gates, live)


def body(
    image_states, w_key, w_value, key_gain, query_gain, head_gate, queries, tile_counts, owner_of
):
    own_index = lax.axis_index("dec")
    tiles_total = image_states.shape[0]
    head_size = key_gain.shape[0]
    kv_heads = w_key.shape[1] // head_size
    request_ids = jnp.arange(owner_of.shape[0], dtype=jnp.int32)
    owned = owner_of[None, :] == request_ids[:, None]
    tile_starts = jnp.cumsum(tile_counts) - tile_counts
    peer_counts = jnp.sum(jnp.where(owned, tile_counts[None, :], 0), axis=1)
    peer_starts = jnp.sum(jnp.where(owned, tile_starts[None, :], 0), axis=1)
    slot_ids = jnp.arange(MAX_TILES, dtype=jnp.int32)
    wanted = jnp.minimum(peer_starts[None, :] + slot_ids[:, None], tiles_total - 1)
    in_use = slot_ids[:, None] < peer_counts[None, :]

    def pack(source):
        picked = jnp.take(source, wanted, axis=0)
        return jnp.where(in_use[:, :, None, None], picked, jnp.zeros((), source.dtype))

    own_count = jnp.sum(jnp.where(request_ids == own_index, peer_counts, 0))
    key_rows, value_rows = project_rows(image_states, w_key, w_value, key_gain, kv_heads)
    outgoing = (pack(key_rows), pack(value_rows))
    received = (
        lax.all_to_all(outgoing[0], "dec", split_axis=1, concat_axis=1, tiled=True),
        lax.all_to_all(outgoing[1], "dec", split_axis=1, concat_axis=1, tiled=True),
    )
    slot_live = (slot_ids < own_count).astype(jnp.float32)
    gates = jnp.repeat(jnp.tanh(head_gate), head_size)[None, :]
    width = kv_heads * head_size
    mixed = attend(
        queries[0],
        received[0].reshape(-1, width),
        received[1].reshape(-1, width),
        query_gain[None, :],
        gates,
        slot_live,
        head_size,
    )
    return mixed[None]


def solution(mesh):
    placed = (
        P("group", "dec", None),
        P("dec", None),
        P("dec", None),
        P(),
        P(),
        P(),
        P(("group", "dec"), None, None),
        P("group"),
        P("group"),
    )
    return jax.shard_map(
        body, mesh=mesh, in_specs=placed, out_specs=P(("group", "dec"), None, None), check_vma=False
    )
```

time: 292 us -> 256 us (0.88)
  matrix products: 41.3 us -> 17.5 us
  other arithmetic: 26 us -> 5.87 us
  Pallas kernels: 0 us -> 11.9 us
  local copies, waits for them, and re-layouts: 29.2 us -> 21.8 us
  waiting for transfers between devices: 170 us -> 175 us
    dot_general x8 -> x0, matrix products: 23.9 us -> none  [the longest x4 14.1 us: one_head(): jnp.einsum('mgtk,mkh->mtgh', weights.astype(jnp.bfloat16), value_part, pr...]
    pallas_call x0 -> x1, Pallas kernels: none -> 11.9 us  [attend(): pl.pallas_call(functools.partial(attend_kernel, scale, head_size), grid=(...]
    reduce_sum x3 -> x0, other arithmetic: 10.9 us -> none  [the longest x1 10.3 us: body(): accum_sum = jnp.sum(accum * slot_live[:, None, None, None, None], axis=0)]
    div x1 -> x0, local copies, waits for them, and re-layouts: 5.61 us -> none  [body(): accum_sum / jnp.transpose(total_sum, (2, 0, 1))[:, :, :, None]]
    all_to_all x1, waiting for transfers between devices: 17 us -> 22.6 us  [body(): lax.all_to_all(outgoing[1], 'dec', split_axis=1, concat_axis=1, tiled=True)]
    div x1 -> x0, other arithmetic: 4.64 us -> none  [body(): accum_sum / jnp.transpose(total_sum, (2, 0, 1))[:, :, :, None]]
    convert_element_type x1 -> x0, other arithmetic: 3.88 us -> none  [body(): mixed.reshape(text_len, kv_heads * group_size * head_size)]
    unnamed x7 -> x10, local copies, waits for them, and re-layouts: 3.29 us -> 0.02 us
where the time goes in v1:
time: 256 us
  waiting for transfers between devices  175 us (68%)
  local copies, waits for them, and re-layouts  21.8 us (9%)
  matrix products  17.5 us (7%)
  between operations  13.5 us (5%)
  Pallas kernels  11.9 us (5%)
  starting transfers between devices  10.4 us (4%)
  other arithmetic  5.87 us (2%)
    all_gather x1, waiting for transfers between devices, project_rows(): lax.all_gather(w_key, 'dec', axis=0, tiled=True)  74 us
    all_gather x1, waiting for transfers between devices, project_rows(): lax.all_gather(w_value, 'dec', axis=0, tiled=True)  54.3 us
    all_to_all x1, waiting for transfers between devices, body(): lax.all_to_all(outgoing[1], 'dec', split_axis=1, concat_axis=1, tiled=True)  22.6 us
    all_to_all x1, waiting for transfers between devices, body(): lax.all_to_all(outgoing[0], 'dec', split_axis=1, concat_axis=1, tiled=True)  22.4 us
    dot_general x1, local copies, waits for them, and re-layouts, project_rows(): jnp.dot(flat_rows, lax.all_gather(w_key, 'dec', axis=0, tiled=True), pref...  12.1 us
    pallas_call x1, Pallas kernels, attend(): pl.pallas_call(functools.partial(attend_kernel, scale, head_size), grid=(...  11.9 us
    dot_general x1, matrix products, project_rows(): jnp.dot(flat_rows, lax.all_gather(w_value, 'dec', axis=0, tiled=True), pr...  9.41 us
    dot_general x1, matrix products, project_rows(): jnp.dot(flat_rows, lax.all_gather(w_key, 'dec', axis=0, tiled=True), pref...  8.05 us
  transfers between devices with their start and end apart: 4, of which 4 were waited for; matrix products, arithmetic and copies ran while one was open for 11% of the time, Pallas kernels for 0%

profile of v1, /device:TPU:11, one launch (start us, length us, event | category | flops | bytes accessed | tf_op | source)
XLA Modules:
  0.0 255.6 jit_solution(5429241782396026283)
XLA Ops:
  6.5 0.7 all-gather.3.cloned.1.call-update
  7.3 0.0 all-gather.5.cloned.1.call-start
  7.3 0.7 all-gather.5.cloned.1.call-update
  8.0 0.7 copy.30
  8.8 0.1 reduce
  8.9 0.7 sub.3
  9.6 0.8 select_reduce_fusion.1
  10.4 0.1 reshape.106
  10.5 74.0 %all-gather.3.cloned.1.call-done = bf16[8192,512]{1,0:T(8,128)(2,1)} async-done(((bf16[512,512]{1,0:T(8,128)(2,1)}), bf16[8192,512]{1,0:T(8,128)(2,1)}) %all-gather.3.cloned.1.call-update) | async-done | bytes 8388624 | tf_op jit(solution)/shard_map/all_gather | solution.py:29
  84.5 12.1 %copy.31 = bf16[512,8192]{1,0:T(8,128)(2,1)} copy(bf16[512,8192]{0,1:T(8,128)(2,1)} %bitcast.24) | data formatting | bytes 16777216 | tf_op jit(solution)/shard_map/dot_general | solution.py:27
  96.6 8.1 %multiply_reduce_fusion = (f32[448,4]{0,1:T(4,128)S(1)}, f32[448,4,128]{2,0,1:T(8,128)S(1)}) fusion(bf16[448,8192,1]{1,0,2:T(8,128)(2,1)} %bitcast.30, bf16[4,128,8192]{2,1,0:T(8,128)(2,1)} %bitcast.25), kind=kOutput, calls=%fused_computation.6 | convolution fusion | flops 3758553344 | bytes 16653312 | tf_op jit(solution)/shard_map/dot_general | solution.py:27
  104.7 0.3 multiply_convert_fusion
  105.0 0.4 copy.32
  105.4 0.2 reshape.80
  105.6 54.3 %all-gather.5.cloned.1.call-done = bf16[8192,512]{1,0:T(8,128)(2,1)} async-done(((bf16[512,512]{1,0:T(8,128)(2,1)}), bf16[8192,512]{1,0:T(8,128)(2,1)}) %all-gather.5.cloned.1.call-update) | async-done | bytes 8388624 | tf_op jit(solution)/shard_map/all_gather | solution.py:34
  159.8 9.4 %convolution_convert_fusion = bf16[448,512]{1,0:T(8,128)(2,1)S(1)} fusion(bf16[448,8192]{1,0:T(8,128)(2,1)} %bitcast.31, bf16[8192,512]{1,0:T(8,128)(2,1)} %all-gather.5.cloned.1.call-done), kind=kOutput, calls=%fused_computation.2 | convolution fusion | flops 3758325760 | bytes 16187392 | tf_op jit(solution)/shard_map/dot_general | solution.py:32
  169.3 0.0 copy-start.4
  169.3 0.6 gather_fusion.1
  169.9 1.6 gather_fusion
  171.5 2.7 %select_select_fusion = (bf16[4,16,16,512]{3,2,1,0:T(8,128)(2,1)S(1)}, bf16[4,16,16,512]{3,2,1,0:T(8,128)(2,1)}) fusion(bf16[4,16,16,512]{3,2,1,0:T(8,128)(2,1)S(1)} %bitcast.26, pred[4,16]{1,0:T(4,128)(4,1)S(1)} %get-tuple-element.13, pred[4,16]{1,0:T(4,128)(4,1)S(1)} %get-tuple-element.12, bf16[4,16,16,512]{3,2,1,0:T(8,128)(2,1)} %bitcast.27), kind=kLoop, calls=%fused_computation.3 | loop fusion | flops 2097152 | bytes 4194432 | tf_op jit(solution)/shard_map/jit(_where)/select_n | solution.py:112
  174.1 1.1 copy.35
  175.3 5.4 %all-to-all-start.1 = ((bf16[4,16,16,512]{3,2,0,1:T(8,128)(2,1)}), bf16[4,16,16,512]{3,2,0,1:T(8,128)(2,1)S(1)}, u32[]{:S(2)}, u32[]{:S(2)}) async-start(bf16[4,16,16,512]{3,2,0,1:T(8,128)(2,1)} %copy.35), calls=%async_computation.1 | async-start | bytes 2097152 | tf_op jit(solution)/shard_map/all_to_all | solution.py:119
  180.7 2.3 copy.33
  183.0 22.6 %all-to-all-done.1 = bf16[4,16,16,512]{3,2,0,1:T(8,128)(2,1)S(1)} async-done(((bf16[4,16,16,512]{3,2,0,1:T(8,128)(2,1)}), bf16[4,16,16,512]{3,2,0,1:T(8,128)(2,1)S(1)}, u32[]{:S(2)}, u32[]{:S(2)}) %all-to-all-start.1) | async-done | bytes 1048608 | tf_op jit(solution)/shard_map/all_to_all | solution.py:119
  205.6 4.9 %all-to-all-start = ((bf16[4,16,16,512]{3,2,0,1:T(8,128)(2,1)}), bf16[4,16,16,512]{3,2,0,1:T(8,128)(2,1)}, u32[]{:S(2)}, u32[]{:S(2)}) async-start(bf16[4,16,16,512]{3,2,0,1:T(8,128)(2,1)} %copy.33), calls=%async_computation | async-start | bytes 2097152 | tf_op jit(solution)/shard_map/all_to_all | solution.py:118
  210.5 0.6 fusion
  211.1 0.6 compare_convert_fusion.live_ref
  211.8 1.3 copy.36
  213.1 22.4 %all-to-all-done = bf16[4,16,16,512]{3,2,0,1:T(8,128)(2,1)} async-done(((bf16[4,16,16,512]{3,2,0,1:T(8,128)(2,1)}), bf16[4,16,16,512]{3,2,0,1:T(8,128)(2,1)}, u32[]{:S(2)}, u32[]{:S(2)}) %all-to-all-start) | async-done | bytes 1048608 | tf_op jit(solution)/shard_map/all_to_all | solution.py:118
  235.5 1.3 copy.34
  236.8 0.1 broadcast_in_dim.74
  236.8 11.9 %shard_map.91 = bf16[256,4096]{1,0:T(8,128)(2,1)} custom-call(bf16[256,4096]{1,0:T(8,128)(2,1)S(1)} %bitcast.21, bf16[1024,512]{1,0:T(8,128)(2,1)S(1)} %bitcast.20, bf16[1024,512]{1,0:T(8,128)(2,1)S(1)} %bitcast.19, f32[1,128]{1,0:T(1,128)S(1)} %bitcast.23, f32[1,4096]{1,0:T(1,128)S(1)} %bitcast.22, f32[4]{0:T(128)S(1)} %compare_convert_fusion.live_ref), custom_call_target="tpu_custom_call" | custom-call | tf_op jit(solution)/shard_map/pallas_call | solution.py:77
  (16 shorter events, 0.1 us)
Async XLA Ops:
  6.5 78.0 %all-gather.3.cloned.1.call-start = ((), (), s32[]{:S(2)}) async-start(), calls=%async_computation.2 | async-start | bytes 8912896 | tf_op jit(solution)/shard_map/all_gather | solution.py:29
  7.3 152.6 %all-gather.5.cloned.1.call-start = ((), (), s32[]{:S(2)}) async-start(), calls=%async_computation.3 | async-start | bytes 8912896 | tf_op jit(solution)/shard_map/all_gather | solution.py:34
  96.6 8.1 %copy-start.3 = (f32[128]{0:T(128)S(1)}, f32[128]{0:T(128)}, u32[]{:S(2)}) copy-start(f32[128]{0:T(128)} %param.14) | copy-start | bytes 1540
  169.3 41.2 %copy-start.4 = (f32[32]{0:T(128)S(1)}, f32[32]{0:T(128)}, u32[]{:S(2)}) copy-start(f32[32]{0:T(128)} %param.16) | copy-start | bytes 388
  171.5 65.4 %copy-start = (bf16[1,256,4096]{2,1,0:T(8,128)(2,1)S(1)}, bf16[1,256,4096]{2,1,0:T(8,128)(2,1)}, u32[]{:S(2)}) copy-start(bf16[1,256,4096]{2,1,0:T(8,128)(2,1)} %param.17) | copy-start | bytes 6291460
  171.5 65.4 %copy-start.1 = (f32[128]{0:T(128)S(1)}, f32[128]{0:T(128)}, u32[]{:S(2)}) copy-start(f32[128]{0:T(128)} %param.15) | copy-start | bytes 1540
  175.3 30.3 %all-to-all-start.1 = ((bf16[4,16,16,512]{3,2,0,1:T(8,128)(2,1)}), bf16[4,16,16,512]{3,2,0,1:T(8,128)(2,1)S(1)}, u32[]{:S(2)}, u32[]{:S(2)}) async-start(bf16[4,16,16,512]{3,2,0,1:T(8,128)(2,1)} %copy.35), calls=%async_computation.1 | async-start | bytes 2097152 | tf_op jit(solution)/shard_map/all_to_all | solution.py:119
  205.6 4.9 %copy-start.2 = (bf16[4,16,16,512]{3,2,0,1:T(8,128)(2,1)}, bf16[4,16,16,512]{3,2,0,1:T(8,128)(2,1)S(1)}, u32[]{:S(2)}) copy-start(bf16[4,16,16,512]{3,2,0,1:T(8,128)(2,1)S(1)} %all-to-all-done.1) | copy-start | bytes 3145732
  205.6 29.9 %all-to-all-start = ((bf16[4,16,16,512]{3,2,0,1:T(8,128)(2,1)}), bf16[4,16,16,512]{3,2,0,1:T(8,128)(2,1)}, u32[]{:S(2)}, u32[]{:S(2)}) async-start(bf16[4,16,16,512]{3,2,0,1:T(8,128)(2,1)} %copy.33), calls=%async_computation | async-start | bytes 2097152 | tf_op jit(solution)/shard_map/all_to_all | solution.py:118
Sparse Core Ops, SparseCore 0:
  9.5 74.9 all-gather.2
  86.7 73.1 all-gather.4

commit v2 on v1

--- a/solution.py
+++ b/solution.py
@@ -68,10 +68,10 @@
         o_ref[:, cols] = (acc[:, :head_size] / acc[:, head_size:] * gate).astype(o_ref.dtype)
 
 
-def attend(queries, keys, values, query_gain, gates, live, head_size):
+def attend(queries, routed, query_gain, gates, live, head_size):
     text_len, width = queries.shape
-    total = keys.shape[0]
-    kv_heads = keys.shape[1] // head_size
+    total = routed.shape[1]
+    kv_heads = routed.shape[2] // head_size
     part = width // kv_heads
     scale = math.log2(math.e) / math.sqrt(head_size)
     return pl.pallas_call(
@@ -80,19 +80,388 @@
         out_shape=jax.ShapeDtypeStruct((text_len, width), jnp.bfloat16),
         in_specs=[
             pl.BlockSpec((text_len, part), lambda h: (0, h)),
-            pl.BlockSpec((total, head_size), lambda h: (0, h)),
-            pl.BlockSpec((total, head_size), lambda h: (0, h)),
+            pl.BlockSpec((None, total, head_size), lambda h: (0, 0, h)),
+            pl.BlockSpec((None, total, head_size), lambda h: (1, 0, h)),
             pl.BlockSpec((1, head_size), lambda h: (0, 0)),
             pl.BlockSpec((1, part), lambda h: (0, h)),
             pl.BlockSpec(memory_space=pltpu.SMEM),
         ],
         out_specs=pl.BlockSpec((text_len, part), lambda h: (0, h)),
         compiler_params=pltpu.CompilerParams(vmem_limit_bytes=32 << 20),
-    )(queries, keys, values, query_gain, gates, live)
+    )(queries, routed, routed, query_gain, gates, live)
+
+
+PIECES = 8
+Z_PIECES = 6
+X_PIECES = 5
+Z_SIZE = 4
+
+
+def route_kernel(
+    head_size,
+    x_hbm,
+    wk_hbm,
+    wv_hbm,
+    kgain_ref,
+    wanted_ref,
+    out_ref,
+    x_buf,
+    w_buf,
+    acc,
+    kv_buf,
+    pack,
+    load_sem,
+    z_recv,
+    x_recv,
+    ya_recv,
+    yb_recv,
+    sib_recv,
+    zup_send,
+    zdn_send,
+    x_send,
+    ya_send,
+    yb_send,
+    sib_send,
+    a2a_send,
+    a2a_recv,
+    own_sem,
+):
+    me = lax.axis_index("dec")
+    y = lax.axis_index("group")
+    devices = pack.shape[1]
+    slots = pack.shape[0]
+    z, x, c = me // 4, (me // 2) % 2, me % 2
+    rows, depth, width = w_buf.shape[1], w_buf.shape[1] * PIECES // 2, w_buf.shape[2]
+    sib = {"dec": me + 1 - 2 * c}
+    x_peer = {"dec": me + 2 - 4 * x}
+    y_peer = {"group": 1 - y}
+    up = {"dec": lax.rem(me + 4, devices)}
+    down = {"dec": lax.rem(me + devices - 4, devices)}
+
+    half = PIECES // 2
+    loads = [
+        pltpu.make_async_copy(x_hbm, x_buf, load_sem.at[0]),
+    ]
+    for i in range(half):
+        part = pl.ds(i * rows, rows)
+        loads.append(
+            pltpu.make_async_copy(
+                wk_hbm.at[part, :], w_buf.at[me * PIECES + i], load_sem.at[1 + i]
+            )
+        )
+        loads.append(
+            pltpu.make_async_copy(
+                wv_hbm.at[part, :], w_buf.at[me * PIECES + half + i], load_sem.at[1 + half + i]
+            )
+        )
+    for load in loads[1:]:
+        load.start()
+    loads[0].start()
+
+    barrier = pltpu.get_barrier_semaphore()
+
+    @pl.loop(1, devices)
+    def _(i):
+        pl.semaphore_signal(
+            barrier,
+            inc=1,
+            device_id={"dec": lax.rem(me + i, devices)},
+            device_id_type=pl.DeviceIdType.MESH,
+        )
+
+    pl.semaphore_signal(barrier, inc=1, device_id=y_peer, device_id_type=pl.DeviceIdType.MESH)
+    pl.semaphore_wait(barrier, devices)
+
+    def shard_of(zs, xs, cs):
+        return (zs * 2 + xs) * 2 + cs
+
+    def move(first, count, send_sem, recv_sem, peer):
+        part = w_buf.at[pl.ds(first, count)]
+        return pltpu.make_async_remote_copy(
+            src_ref=part,
+            dst_ref=part,
+            send_sem=send_sem,
+            recv_sem=recv_sem,
+            device_id=peer,
+            device_id_type=pl.DeviceIdType.MESH,
+        )
+
+    def piece(q):
+        return q + y * (PIECES - 1 - 2 * q)
+
+    def near(zs):
+        return zs * 2 + x
+
+    def far(zs):
+        return zs * 2 + 1 - x
+
+    def to_up(zs, q):
+        return move(
+            shard_of(zs, x, c) * PIECES + piece(q), 1, zup_send.at[zs], z_recv.at[zs, q], up
+        )
+
+    def to_down(zs, q):
+        return move(
+            shard_of(zs, x, c) * PIECES + piece(q), 1, zdn_send.at[zs], z_recv.at[zs, q], down
+        )
+
+    def to_x(zs, q):
+        return move(
+            shard_of(zs, x, c) * PIECES + piece(q), 1, x_send.at[zs], x_recv.at[zs, q], x_peer
+        )
+
+    def to_sib(zs, xs, first, count):
+        index = zs * 2 + xs
+        return move(
+            shard_of(zs, xs, c) * PIECES + first, count, sib_send.at[index], sib_recv.at[index], sib
+        )
+
+    for load in loads[1:]:
+        load.wait()
+
+    @pl.loop(0, PIECES)
+    def _(q):
+        @pl.when(q < Z_PIECES)
+        def _():
+            @pl.when(z < Z_SIZE - 1)
+            def _():
+                to_up(z, q).start()
+
+            @pl.when(z > 0)
+            def _():
+                to_down(z, q).start()
+
+        @pl.when(q < X_PIECES)
+        def _():
+            to_x(z, q).start()
+
+    to_sib(z, x, 0, PIECES).start()
+    acc[...] = jnp.zeros_like(acc)
+    loads[0].wait()
+
+    def in_line(step, low, d):
+        zs = z + (2 * d - 1) * step
+        ok = (step >= low) & (step < Z_SIZE) & (zs >= 0) & (zs < Z_SIZE)
+        return zs, ok & ((d == 0) | (step > 0))
+
+    a_late = PIECES - Z_PIECES
+    b_late = PIECES - X_PIECES
+
+    @pl.loop(0, Z_SIZE + 2)
+    def _(t):
+        for d in range(2):
+            zs, ok = in_line(t - 1, 1, d)
+
+            @pl.when(ok)
+            def _():
+                first = Z_PIECES * (1 - y)
+                base = shard_of(zs, x, c) * PIECES
+                move(base + first, a_late, ya_send.at[zs], ya_recv.at[zs], y_peer).wait_recv()
+                to_sib(zs, x, first, a_late).start()
+
+            zb, okb = in_line(t - 2, 0, d)
+
+            @pl.when(okb)
+            def _():
+                first = X_PIECES * (1 - y)
+                base = shard_of(zb, 1 - x, c) * PIECES
+                move(base + first, b_late, yb_send.at[zb], yb_recv.at[zb], y_peer).wait_recv()
+                to_sib(zb, 1 - x, first, b_late).start()
+
+        @pl.loop(0, PIECES)
+        def _(q):
+            for d in range(2):
+                zs, ok = in_line(t, 1, d)
+
+                @pl.when(ok & (q < Z_PIECES))
+                def _():
+                    if d == 0:
+                        to_up(zs, q).wait_recv()
+
+                        @pl.when(z < Z_SIZE - 1)
+                        def _():
+                            to_up(zs, q).start()
+                    else:
+                        to_down(zs, q).wait_recv()
+
+                        @pl.when(z > 0)
+                        def _():
+                            to_down(zs, q).start()
+
+                    @pl.when(q < X_PIECES)
+                    def _():
+                        to_x(zs, q).start()
+
+                    @pl.when(q < a_late)
+                    def _():
+                        move(
+                            shard_of(zs, x, c) * PIECES + piece(q),
+                            1,
+                            ya_send.at[zs],
+                            ya_recv.at[zs],
+                            y_peer,
+                        ).start()
+
+                    to_sib(zs, x, piece(q), 1).start()
+
+                zb, okb = in_line(t - 1, 0, d)
+
+                @pl.when(okb & (q < X_PIECES))
+                def _():
+                    first = shard_of(zb, 1 - x, c) * PIECES + piece(q)
+                    move(first, 1, x_send.at[zb], x_recv.at[zb, q], x_peer).wait_recv()
+
+                    @pl.when(q < b_late)
+                    def _():
+                        move(first, 1, yb_send.at[zb], yb_recv.at[zb], y_peer).start()
+
+                    to_sib(zb, 1 - x, piece(q), 1).start()
+
+            other = q // 4
+            is_far = (q // 2) % 2
+            d = q % 2
+            zm, okm = in_line(t - 1 - is_far, 0, d)
+
+            @pl.when(okm)
+            def _():
+                xm = x + is_far * (1 - 2 * x)
+                cm = c + other * (1 - 2 * c)
+
+                @pl.when(other == 1)
+                def _():
+                    index = zm * 2 + xm
+                    move(
+                        shard_of(zm, xm, cm) * PIECES,
+                        PIECES,
+                        sib_send.at[index],
+                        sib_recv.at[index],
+                        sib,
+                    ).wait_recv()
+
+                shard = shard_of(zm, xm, cm)
+                cols = pl.ds(pl.multiple_of(shard * depth, depth), depth)
+                for k in range(2):
+                    block = w_buf[pl.ds(shard * PIECES + k * half, half)].reshape(depth, width)
+                    out = pl.ds(k * width, width)
+                    acc[:, out] += jnp.dot(
+                        x_buf[:, cols], block, preferred_element_type=jnp.float32
+                    )
+
+    tiles = kv_buf.shape[0]
+    tokens = kv_buf.shape[2]
+    for h in range(width // head_size):
+        cols = pl.ds(h * head_size, head_size)
+        keys = rms_scale(acc[:, cols], kgain_ref[...]).astype(jnp.bfloat16)
+        kv_buf[:, 0, :, cols] = keys.reshape(tiles, tokens, head_size)
+    kv_buf[:, 1, :, :] = acc[:, width:].astype(jnp.bfloat16).reshape(tiles, tokens, width)
+
+    def exchange(j, dest):
+        return pltpu.make_async_remote_copy(
+            src_ref=pack.at[j, dest],
+            dst_ref=out_ref.at[:, j, me],
+            send_sem=a2a_send.at[j],
+            recv_sem=a2a_recv.at[j],
+            device_id={"dec": dest},
+            device_id_type=pl.DeviceIdType.MESH,
+        )
+
+    @pl.loop(0, slots)
+    def _(j):
+        @pl.loop(1, devices)
+        def _(i):
+            dest = lax.rem(me + i, devices)
+            pack[j, dest] = kv_buf[wanted_ref[j, dest]]
+            exchange(j, dest).start()
+
+        pack[j, me] = kv_buf[wanted_ref[j, me]]
+        pltpu.make_async_copy(pack.at[j, me], out_ref.at[:, j, me], own_sem.at[j]).start()
+
+    for zs in range(Z_SIZE):
+
+        @pl.when((z >= zs) & (z < Z_SIZE - 1))
+        def _():
+            move(zs * PIECES, Z_PIECES, zup_send.at[zs], z_recv.at[zs, 0], up).wait_send()
+
+        @pl.when((z <= zs) & (z > 0))
+        def _():
+            move(zs * PIECES, Z_PIECES, zdn_send.at[zs], z_recv.at[zs, 0], down).wait_send()
+
+        move(zs * PIECES, X_PIECES, x_send.at[zs], x_recv.at[zs, 0], x_peer).wait_send()
+
+        @pl.when(z != zs)
+        def _():
+            move(zs * PIECES, a_late, ya_send.at[zs], ya_recv.at[zs], y_peer).wait_send()
+
+        move(zs * PIECES, b_late, yb_send.at[zs], yb_recv.at[zs], y_peer).wait_send()
+        for xs in range(2):
+            to_sib(zs, xs, 0, PIECES).wait_send()
+
+    for j in range(slots):
+        pltpu.make_async_copy(pack.at[j, me], out_ref.at[:, j, me], own_sem.at[j]).wait()
+        whole = pltpu.make_async_remote_copy(
+            src_ref=pack.at[j, pl.ds(0, devices - 1)],
+            dst_ref=pack.at[j, pl.ds(0, devices - 1)],
+            send_sem=a2a_send.at[j],
+            recv_sem=a2a_recv.at[j],
+            device_id=sib,
+            device_id_type=pl.DeviceIdType.MESH,
+        )
+        whole.wait_send()
+        whole.wait_recv()
+
+
+def project_and_route(states, w_key, w_value, key_gain, wanted):
+    tiles, tokens, model = states.shape
+    slots, devices = wanted.shape
+    depth, width = w_key.shape
+    head_size = key_gain.shape[0]
+    flat = tiles * tokens
+    shards = devices // 2
+    dma = pltpu.SemaphoreType.DMA
+    return pl.pallas_call(
+        functools.partial(route_kernel, head_size),
+        out_shape=jax.ShapeDtypeStruct((2, slots, devices, tokens, width), jnp.bfloat16),
+        in_specs=[
+            pl.BlockSpec(memory_space=pl.ANY),
+            pl.BlockSpec(memory_space=pl.ANY),
+            pl.BlockSpec(memory_space=pl.ANY),
+            pl.BlockSpec(memory_space=pltpu.VMEM),
+            pl.BlockSpec(memory_space=pltpu.SMEM),
+        ],
+        out_specs=pl.BlockSpec(memory_space=pl.ANY),
+        scratch_shapes=[
+            pltpu.VMEM((flat, model), jnp.bfloat16),
+            pltpu.VMEM((devices * PIECES, 2 * depth // PIECES, width), jnp.bfloat16),
+            pltpu.VMEM((flat, 2 * width), jnp.float32),
+            pltpu.VMEM((tiles, 2, tokens, width), jnp.bfloat16),
+            pltpu.VMEM((slots, devices, 2, tokens, width), jnp.bfloat16),
+            dma((1 + PIECES,)),
+            dma((Z_SIZE, Z_PIECES)),
+            dma((Z_SIZE, X_PIECES)),
+            dma((Z_SIZE,)),
+            dma((Z_SIZE,)),
+            dma((shards,)),
+            dma((Z_SIZE,)),
+            dma((Z_SIZE,)),
+            dma((Z_SIZE,)),
+            dma((Z_SIZE,)),
+            dma((Z_SIZE,)),
+            dma((shards,)),
+            dma((slots,)),
+            dma((slots,)),
+            dma((slots,)),
+        ],
+        compiler_params=pltpu.CompilerParams(
+            collective_id=0, has_side_effects=True, vmem_limit_bytes=48 << 20
+        ),
+        cost_estimate=pl.CostEstimate(
+            flops=4 * flat * model * width, bytes_accessed=40 << 20, transcendentals=0
+        ),
+    )(states.reshape(flat, model), w_key, w_value, key_gain[None, :], wanted)
 
 
 def body(
-    image_states, w_key, w_value, key_gain, query_gain, head_gate, queries, tile_counts, owner_of
+    on_grid, image_states, w_key, w_value, key_gain, query_gain, head_gate, queries, tile_counts, owner_of
 ):
     own_index = lax.axis_index("dec")
     tiles_total = image_states.shape[0]
@@ -105,31 +474,26 @@
     peer_starts = jnp.sum(jnp.where(owned, tile_starts[None, :], 0), axis=1)
     slot_ids = jnp.arange(MAX_TILES, dtype=jnp.int32)
     wanted = jnp.minimum(peer_starts[None, :] + slot_ids[:, None], tiles_total - 1)
-    in_use = slot_ids[:, None] < peer_counts[None, :]
 
     def pack(source):
-        picked = jnp.take(source, wanted, axis=0)
-        return jnp.where(in_use[:, :, None, None], picked, jnp.zeros((), source.dtype))
+        return jnp.take(source, wanted, axis=0)
 
     own_count = jnp.sum(jnp.where(request_ids == own_index, peer_counts, 0))
-    key_rows, value_rows = project_rows(image_states, w_key, w_value, key_gain, kv_heads)
-    outgoing = (pack(key_rows), pack(value_rows))
-    received = (
-        lax.all_to_all(outgoing[0], "dec", split_axis=1, concat_axis=1, tiled=True),
-        lax.all_to_all(outgoing[1], "dec", split_axis=1, concat_axis=1, tiled=True),
-    )
+    width = kv_heads * head_size
+    if on_grid:
+        routed = project_and_route(image_states, w_key, w_value, key_gain, wanted)
+        routed = routed.reshape(2, -1, width)
+    else:
+        rows = project_rows(image_states, w_key, w_value, key_gain, kv_heads)
+        routed = jnp.stack(
+            [
+                lax.all_to_all(pack(part), "dec", split_axis=1, concat_axis=1, tiled=True)
+                for part in rows
+            ]
+        ).reshape(2, -1, width)
     slot_live = (slot_ids < own_count).astype(jnp.float32)
     gates = jnp.repeat(jnp.tanh(head_gate), head_size)[None, :]
-    width = kv_heads * head_size
-    mixed = attend(
-        queries[0],
-        received[0].reshape(-1, width),
-        received[1].reshape(-1, width),
-        query_gain[None, :],
-        gates,
-        slot_live,
-        head_size,
-    )
+    mixed = attend(queries[0], routed, query_gain[None, :], gates, slot_live, head_size)
     return mixed[None]
 
 
@@ -145,6 +509,7 @@
         P("group"),
         P("group"),
     )
+    on_grid = mesh.shape["dec"] == 16 and mesh.shape["group"] == 2
     return jax.shard_map(
-        body, mesh=mesh, in_specs=placed, out_specs=P(("group", "dec"), None, None), check_vma=False
+        functools.partial(body, on_grid), mesh=mesh, in_specs=placed, out_specs=P(("group", "dec"), None, None), check_vma=False
     )

time: 256 us -> 137 us (0.54)
  waiting for transfers between devices: 175 us -> 0 us
  Pallas kernels: 11.9 us -> 129 us
  local copies, waits for them, and re-layouts: 21.8 us -> 4.21 us
  matrix products: 17.5 us -> 0 us
  between operations: 13.5 us -> 0.05 us
  starting transfers between devices: 10.4 us -> 0 us
  other arithmetic: 5.87 us -> 2.89 us
    all_gather x2 -> x0, waiting for transfers between devices: 128 us -> none  [the longest x1 74 us: project_rows(): lax.all_gather(w_key, 'dec', axis=0, tiled=True)]
    pallas_call x0 -> x1, Pallas kernels: none -> 117 us  [project_and_route(): pl.pallas_call(functools.partial(route_kernel, head_size), out_shape=jax....]
    all_to_all x2 -> x0, waiting for transfers between devices: 45 us -> none  [the longest x1 22.6 us: body(): lax.all_to_all(outgoing[1], 'dec', split_axis=1, concat_axis=1, tiled=True)]
    dot_general x2 -> x0, matrix products: 17.5 us -> none  [the longest x1 9.41 us: project_rows(): jnp.dot(flat_rows, lax.all_gather(w_value, 'dec', axis=0, tiled=True), pr...]
    dot_general x1 -> x0, local copies, waits for them, and re-layouts: 12.1 us -> none  [project_rows(): jnp.dot(flat_rows, lax.all_gather(w_key, 'dec', axis=0, tiled=True), pref...]
    all_to_all x2 -> x0, starting transfers between devices: 10.3 us -> none  [the longest x1 5.41 us: body(): lax.all_to_all(outgoing[1], 'dec', split_axis=1, concat_axis=1, tiled=True)]
    select_n x2 -> x0, local copies, waits for them, and re-layouts: 3.41 us -> none  [pack(): jnp.where(in_use[:, :, None, None], picked, jnp.zeros((), source.dtype))]
    unnamed x10, local copies, waits for them, and re-layouts: 0.02 us -> 2.75 us
  transfers between devices with their start and end apart: 4 -> 0, of which waited for: 4 -> 0; matrix products, arithmetic and copies ran while one was open for 11% -> 0% of each run, Pallas kernels for 0% -> 0%
where the time goes in v2:
time: 137 us; the launch traced here: 136 us
  Pallas kernels  129 us (94%)
  local copies, waits for them, and re-layouts  4.21 us (3%)
  other arithmetic  2.89 us (2%)
    pallas_call x1, Pallas kernels, project_and_route(): pl.pallas_call(functools.partial(route_kernel, head_size), out_shape=jax....  117 us
    pallas_call x1, Pallas kernels, attend(): pl.pallas_call(functools.partial(attend_kernel, scale, head_size), grid=(...  11.9 us
    unnamed x10, local copies, waits for them, and re-layouts  2.75 us

profile of v2, /device:TPU:11, one launch (start us, length us, event | category | flops | bytes accessed | tf_op | source)
XLA Modules:
  0.0 136.4 jit_solution(5437639545844163306)
XLA Ops:
  0.0 0.7 tanh.3
  0.7 0.7 copy.12
  1.4 0.1 reduce
  1.6 0.7 sub.3
  2.2 0.8 select_reduce_fusion
  3.0 0.6 fusion
  3.6 0.6 compare_convert_fusion.live_ref
  4.3 0.1 broadcast_in_dim.44
  4.4 0.0 copy-start.2
  4.4 1.0 copy-done.2
  5.4 0.0 copy-start.3
  5.4 1.0 copy-done.3
  6.5 0.0 copy-start.4
  6.5 0.7 copy-done.4
  7.1 0.0 copy-start
  7.1 0.0 copy-start.1
  7.1 117.3 %shard_map.91 = bf16[2,4,16,16,512]{4,3,2,1,0:T(8,128)(2,1)S(1)} custom-call(bf16[448,8192]{1,0:T(8,128)(2,1)} %bitcast.15, bf16[512,512]{1,0:T(8,128)(2,1)S(1)} %copy-done.2, bf16[512,512]{1,0:T(8,128)(2,1)S(1)} %copy-done.3, f32[1,128]{1,0:T(1,128)S(1)} %bitcast.13, s32[4,16]{1,0:T(4,128)S(1)} %add_minimum_fusion.wanted_ref), custom_call_target="tpu_custom_call" | custom-call | flops 7516192768 | bytes 41943040 | tf_op jit(solution)/shard_map/pallas_call | solution.py:421
  124.4 0.0 copy-done
  124.5 0.0 copy-done.1
  124.5 11.9 %shard_map.92 = bf16[256,4096]{1,0:T(8,128)(2,1)} custom-call(bf16[256,4096]{1,0:T(8,128)(2,1)S(1)} %bitcast.10, bf16[2,1024,512]{2,1,0:T(8,128)(2,1)S(1)} %bitcast.8, bf16[2,1024,512]{2,1,0:T(8,128)(2,1)S(1)} %bitcast.9, f32[1,128]{1,0:T(1,128)S(1)} %bitcast.12, f32[1,4096]{1,0:T(1,128)S(1)} %bitcast.11, f32[4]{0:T(128)S(1)} %compare_convert_fusion.live_ref), custom_call_target="tpu_custom_call" | custom-call | tf_op jit(solution)/shard_map/pallas_call | solution.py:77
  (2 shorter events, 0.0 us)
Async XLA Ops:
  4.4 1.0 copy-start.2
  5.4 1.0 copy-start.3
  6.5 0.7 copy-start.4
  7.1 117.3 %copy-start = (bf16[1,256,4096]{2,1,0:T(8,128)(2,1)S(1)}, bf16[1,256,4096]{2,1,0:T(8,128)(2,1)}, u32[]{:S(2)}) copy-start(bf16[1,256,4096]{2,1,0:T(8,128)(2,1)} %param.15) | copy-start | bytes 6291460
  7.1 117.3 %copy-start.1 = (f32[128]{0:T(128)S(1)}, f32[128]{0:T(128)}, u32[]{:S(2)}) copy-start(f32[128]{0:T(128)} %param.13) | copy-start | bytes 1540

commit v3 on v2

--- a/solution.py
+++ b/solution.py
@@ -103,13 +103,26 @@
     wk_hbm,
     wv_hbm,
     kgain_ref,
+    qgain_ref,
+    gate_ref,
+    q_hbm,
     wanted_ref,
+    live_ref,
     out_ref,
     x_buf,
     w_buf,
     acc,
     kv_buf,
     pack,
+    recv0,
+    recv1,
+    recv2,
+    recv3,
+    q_raw,
+    q_buf,
+    mix,
+    gates,
+    small_sem,
     load_sem,
     z_recv,
     x_recv,
@@ -126,6 +139,7 @@
     a2a_recv,
     own_sem,
 ):
+    recv = (recv0, recv1, recv2, recv3)
     me = lax.axis_index("dec")
     y = lax.axis_index("group")
     devices = pack.shape[1]
@@ -157,6 +171,15 @@
     for load in loads[1:]:
         load.start()
     loads[0].start()
+    staged = (
+        (q_hbm, q_raw),
+    )
+    smalls = [
+        pltpu.make_async_copy(source, target, small_sem.at[i])
+        for i, (source, target) in enumerate(staged)
+    ]
+    for small in smalls:
+        small.start()
 
     barrier = pltpu.get_barrier_semaphore()
 
@@ -237,6 +260,8 @@
 
     to_sib(z, x, 0, PIECES).start()
     acc[...] = jnp.zeros_like(acc)
+    for small in smalls:
+        small.wait()
     loads[0].wait()
 
     def in_line(step, low, d):
@@ -358,15 +383,15 @@
     def exchange(j, dest):
         return pltpu.make_async_remote_copy(
             src_ref=pack.at[j, dest],
-            dst_ref=out_ref.at[:, j, me],
+            dst_ref=recv[j].at[me],
             send_sem=a2a_send.at[j],
-            recv_sem=a2a_recv.at[j],
+            recv_sem=a2a_recv.at[j, me],
             device_id={"dec": dest},
             device_id_type=pl.DeviceIdType.MESH,
         )
 
-    @pl.loop(0, slots)
-    def _(j):
+    for j in range(slots):
+
         @pl.loop(1, devices)
         def _(i):
             dest = lax.rem(me + i, devices)
@@ -374,7 +399,24 @@
             exchange(j, dest).start()
 
         pack[j, me] = kv_buf[wanted_ref[j, me]]
-        pltpu.make_async_copy(pack.at[j, me], out_ref.at[:, j, me], own_sem.at[j]).start()
+        pltpu.make_async_copy(pack.at[j, me], recv[j].at[me], own_sem.at[j]).start()
+
+    kv_heads = width // head_size
+    heads = gates.shape[0]
+    group_size = heads // kv_heads
+    span = group_size * head_size
+    keys_per_slot = devices * tokens
+    scale = math.log2(math.e) / math.sqrt(head_size)
+    gate_row = jnp.tanh(gate_ref[...])
+    for k in range(heads):
+        gates[k] = jnp.broadcast_to(gate_row[:, k : k + 1], gates.shape[1:])
+
+    @pl.loop(0, heads)
+    def _(k):
+        cols = pl.ds(pl.multiple_of(k * head_size, head_size), head_size)
+        q = rms_scale(q_raw[:, cols].astype(jnp.float32), qgain_ref[...])
+        q_buf[:, cols] = q.astype(jnp.bfloat16)
+        mix[k] = jnp.zeros(mix.shape[1:], mix.dtype)
 
     for zs in range(Z_SIZE):
 
@@ -396,45 +438,98 @@
         for xs in range(2):
             to_sib(zs, xs, 0, PIECES).wait_send()
 
+    def arrived(j):
+        pltpu.make_async_copy(pack.at[j, me], recv[j].at[me], own_sem.at[j]).wait()
+
+        @pl.loop(1, devices)
+        def _(i):
+            source = lax.rem(me + i, devices)
+            pltpu.make_async_remote_copy(
+                src_ref=pack.at[j, source],
+                dst_ref=recv[j].at[source],
+                send_sem=a2a_send.at[j],
+                recv_sem=a2a_recv.at[j, source],
+                device_id={"dec": source},
+                device_id_type=pl.DeviceIdType.MESH,
+            ).wait_recv()
+
+    def attend_slot(j, last):
+        arrived(j)
+        live = live_ref[j]
+        ones = jnp.ones((keys_per_slot, head_size), jnp.bfloat16)
+
+        @pl.loop(0, kv_heads)
+        def _(h):
+            head = pl.ds(pl.multiple_of(h * head_size, head_size), head_size)
+            keys = recv[j][:, 0, :, head].reshape(keys_per_slot, head_size)
+            values = recv[j][:, 1, :, head].reshape(keys_per_slot, head_size)
+            values = jnp.concatenate([values, ones], axis=1)
+            for g in range(group_size):
+                k = h * group_size + g
+                cols = pl.ds(pl.multiple_of(k * head_size, head_size), head_size)
+                scores = lax.dot_general(
+                    q_buf[:, cols],
+                    keys,
+                    (((1,), (1,)), ((), ())),
+                    preferred_element_type=jnp.float32,
+                )
+                weights = jnp.exp2(scores * scale).astype(jnp.bfloat16)
+                part = jnp.dot(weights, values, preferred_element_type=jnp.float32)
+                part = mix[k] + part * live
+                if last:
+                    ratio = part[:, :head_size] / part[:, head_size:] * gates[k][:1]
+                    out_ref[:, cols] = ratio.astype(out_ref.dtype)
+                else:
+                    mix[k] = part
+
     for j in range(slots):
-        pltpu.make_async_copy(pack.at[j, me], out_ref.at[:, j, me], own_sem.at[j]).wait()
-        whole = pltpu.make_async_remote_copy(
+        attend_slot(j, j == slots - 1)
+    for j in range(slots):
+        pltpu.make_async_remote_copy(
             src_ref=pack.at[j, pl.ds(0, devices - 1)],
-            dst_ref=pack.at[j, pl.ds(0, devices - 1)],
+            dst_ref=recv[j].at[pl.ds(0, devices - 1)],
             send_sem=a2a_send.at[j],
-            recv_sem=a2a_recv.at[j],
+            recv_sem=a2a_recv.at[j, 0],
             device_id=sib,
             device_id_type=pl.DeviceIdType.MESH,
-        )
-        whole.wait_send()
-        whole.wait_recv()
-
-
-def project_and_route(states, w_key, w_value, key_gain, wanted):
+        ).wait_send()
+
+
+def attend_on_grid(
+    states, w_key, w_value, key_gain, query_gain, head_gate, queries, wanted, live
+):
     tiles, tokens, model = states.shape
     slots, devices = wanted.shape
     depth, width = w_key.shape
+    text_len, model_out = queries.shape
+    heads = head_gate.shape[0]
     head_size = key_gain.shape[0]
     flat = tiles * tokens
     shards = devices // 2
     dma = pltpu.SemaphoreType.DMA
     return pl.pallas_call(
         functools.partial(route_kernel, head_size),
-        out_shape=jax.ShapeDtypeStruct((2, slots, devices, tokens, width), jnp.bfloat16),
-        in_specs=[
-            pl.BlockSpec(memory_space=pl.ANY),
-            pl.BlockSpec(memory_space=pl.ANY),
-            pl.BlockSpec(memory_space=pl.ANY),
-            pl.BlockSpec(memory_space=pltpu.VMEM),
-            pl.BlockSpec(memory_space=pltpu.SMEM),
-        ],
-        out_specs=pl.BlockSpec(memory_space=pl.ANY),
+        out_shape=jax.ShapeDtypeStruct((text_len, model_out), jnp.bfloat16),
+        in_specs=[pl.BlockSpec(memory_space=pl.ANY)] * 3
+        + [pl.BlockSpec(memory_space=pltpu.VMEM)] * 3
+        + [pl.BlockSpec(memory_space=pl.ANY)]
+        + [pl.BlockSpec(memory_space=pltpu.SMEM)] * 2,
+        out_specs=pl.BlockSpec(memory_space=pltpu.VMEM),
         scratch_shapes=[
             pltpu.VMEM((flat, model), jnp.bfloat16),
             pltpu.VMEM((devices * PIECES, 2 * depth // PIECES, width), jnp.bfloat16),
             pltpu.VMEM((flat, 2 * width), jnp.float32),
             pltpu.VMEM((tiles, 2, tokens, width), jnp.bfloat16),
             pltpu.VMEM((slots, devices, 2, tokens, width), jnp.bfloat16),
+            pltpu.VMEM((devices, 2, tokens, width), jnp.bfloat16),
+            pltpu.VMEM((devices, 2, tokens, width), jnp.bfloat16),
+            pltpu.VMEM((devices, 2, tokens, width), jnp.bfloat16),
+            pltpu.VMEM((devices, 2, tokens, width), jnp.bfloat16),
+            pltpu.VMEM((text_len, model_out), jnp.bfloat16),
+            pltpu.VMEM((text_len, model_out), jnp.bfloat16),
+            pltpu.VMEM((heads, text_len, 2 * head_size), jnp.float32),
+            pltpu.VMEM((heads, 8, head_size), jnp.float32),
+            dma((1,)),
             dma((1 + PIECES,)),
             dma((Z_SIZE, Z_PIECES)),
             dma((Z_SIZE, X_PIECES)),
@@ -448,16 +543,26 @@
             dma((Z_SIZE,)),
             dma((shards,)),
             dma((slots,)),
-            dma((slots,)),
+            dma((slots, devices)),
             dma((slots,)),
         ],
         compiler_params=pltpu.CompilerParams(
-            collective_id=0, has_side_effects=True, vmem_limit_bytes=48 << 20
+            collective_id=0, has_side_effects=True, vmem_limit_bytes=56 << 20
         ),
         cost_estimate=pl.CostEstimate(
             flops=4 * flat * model * width, bytes_accessed=40 << 20, transcendentals=0
         ),
-    )(states.reshape(flat, model), w_key, w_value, key_gain[None, :], wanted)
+    )(
+        states.reshape(flat, model),
+        w_key,
+        w_value,
+        key_gain[None, :],
+        query_gain[None, :],
+        head_gate[None, :],
+        queries,
+        wanted,
+        live,
+    )
 
 
 def body(
@@ -479,19 +584,27 @@
         return jnp.take(source, wanted, axis=0)
 
     own_count = jnp.sum(jnp.where(request_ids == own_index, peer_counts, 0))
+    slot_live = (slot_ids < own_count).astype(jnp.float32)
+    if on_grid:
+        return attend_on_grid(
+            image_states,
+            w_key,
+            w_value,
+            key_gain,
+            query_gain,
+            head_gate,
+            queries[0],
+            wanted,
+            slot_live,
+        )[None]
     width = kv_heads * head_size
-    if on_grid:
-        routed = project_and_route(image_states, w_key, w_value, key_gain, wanted)
-        routed = routed.reshape(2, -1, width)
-    else:
-        rows = project_rows(image_states, w_key, w_value, key_gain, kv_heads)
-        routed = jnp.stack(
-            [
-                lax.all_to_all(pack(part), "dec", split_axis=1, concat_axis=1, tiled=True)
-                for part in rows
-            ]
-        ).reshape(2, -1, width)
-    slot_live = (slot_ids < own_count).astype(jnp.float32)
+    rows = project_rows(image_states, w_key, w_value, key_gain, kv_heads)
+    routed = jnp.stack(
+        [
+            lax.all_to_all(pack(part), "dec", split_axis=1, concat_axis=1, tiled=True)
+            for part in rows
+        ]
+    ).reshape(2, -1, width)
     gates = jnp.repeat(jnp.tanh(head_gate), head_size)[None, :]
     mixed = attend(queries[0], routed, query_gain[None, :], gates, slot_live, head_size)
     return mixed[None]

time: 137 us -> 130 us (0.949)
  Pallas kernels: 129 us -> 122 us
    pallas_call x2 -> x1, Pallas kernels: 129 us -> 122 us  [attend_on_grid(): pl.pallas_call(functools.partial(route_kernel, head_size), out_shape=jax....]
    unnamed x10 -> x1, local copies, waits for them, and re-layouts: 2.75 us -> 3.13 us
where the time goes in v3:
time: 130 us; the launch traced here: 129 us
  Pallas kernels  122 us (94%)
  other arithmetic  3.98 us (3%)
  local copies, waits for them, and re-layouts  3.86 us (3%)
    pallas_call x1, Pallas kernels, attend_on_grid(): pl.pallas_call(functools.partial(route_kernel, head_size), out_shape=jax....  122 us
    unnamed x1, local copies, waits for them, and re-layouts  3.13 us

profile of v3, /device:TPU:11, one launch (start us, length us, event | category | flops | bytes accessed | tf_op | source)
XLA Modules:
  0.0 129.4 jit_solution(16135902699123707067)
XLA Ops:
  0.0 0.7 copy.12
  0.8 0.1 reduce
  0.9 0.7 sub.3
  1.5 0.8 select_reduce_fusion
  2.3 0.6 fusion
  3.0 1.2 compare_convert_fusion.live_ref
  4.1 0.6 add_minimum_fusion.wanted_ref
  4.7 121.6 %shard_map.91 = bf16[256,4096]{1,0:T(8,128)(2,1)} custom-call(bf16[448,8192]{1,0:T(8,128)(2,1)} %bitcast.9, bf16[512,512]{1,0:T(8,128)(2,1)} %wk_hbm.1, bf16[512,512]{1,0:T(8,128)(2,1)} %wv_hbm.1, f32[1,128]{1,0:T(1,128)} %bitcast.11, f32[1,128]{1,0:T(1,128)} %bitcast.12, f32[1,32]{1,0:T(1,128)} %bitcast.13, bf16[256,4096]{1,0:T(8,128)(2,1)} %bitcast.10, ...), custom_call_target="tpu_custom_call" | custom-call | flops 7516192768 | bytes 41943040 | tf_op jit(solution)/shard_map/pallas_call | solution.py:510
  126.3 3.1 %copy.14 = bf16[1,256,4096]{2,1,0:T(8,128)(2,1)} copy(bf16[1,256,4096]{2,1,0:T(8,128)(2,1)} %bitcast.7) | data formatting | bytes 4194304
  (1 shorter events, 0.0 us)
